TPU v7x, 256 devices: a whole 4x4x8 slice. The times are simulated.
256 devices in a mesh: seq: 32 (over x, y, core), chan: 8 (over z).
Axes of the slice: x: 4, y: 4, z: 8, core: 2. Of those that a mesh axis runs over, the one named last changes fastest.
Arguments:
- query_rows: bfloat16 [8192, 8192], P('seq', 'chan'), may hold values from -17 to 17
- key_rows: bfloat16 [8192, 8192], P('seq', 'chan'), may hold values from -6 to 6
- value_rows: bfloat16 [8192, 8192], P('seq', 'chan'), may hold values from -6 to 6
- short_taps: bfloat16 [3, 3, 8192], P(None, None, 'chan'), may hold values from -2.390625 to 2.390625
- medium_taps: bfloat16 [128, 8192], P(None, 'chan'), may hold values from -0.5 to 0.5
- residues: float32 [16, 8192], P(None, 'chan'), may hold values from -0.26 to 0.26
- decay_rates: float32 [16, 8192], P(None, 'chan'), may hold values from 3.6621094e-05 to 0.0333333333
- skip_gain: float32 [8192], P('chan'), may hold values from -3 to 3
- norm_gain: float32 [8192], P('chan'), may hold values from 0.1 to 1.9
Outputs:
- hyena_out: bfloat16 [8192, 8192], P('seq', 'chan')
All inputs are finite; a program needn't handle non-finite values.
Results may differ from a plain program's by a relative error of at most 0.018.
Values may be sent and summed in bfloat16 or wider, within the bound.
A program may use at most 64 MiB of HBM per device.

v0:
```python
import functools
import math

import jax
import jax.numpy as jnp
import ml_dtypes
import numpy as np
from jax import lax
from jax.experimental import pallas as pl
from jax.experimental.pallas import tpu as pltpu
from jax.sharding import PartitionSpec as P

D = 8192
ROWS = 256
TAPS = 128
POLES = 16
LANES = 128
TILE = 256
EDGE = 16
HALF_ONE = 192
HALF_TWO = 256
MESH = pl.DeviceIdType.MESH
BF = jnp.bfloat16
F32 = jnp.float32


def split_np(table):
    high = table.astype(np.float32).astype(ml_dtypes.bfloat16)
    low = (table - high.astype(np.float64)).astype(np.float32).astype(ml_dtypes.bfloat16)
    return np.stack([high, low])


def odd_tables(half, positions):
    angle = (2.0 * math.pi / (2 * half)) * (np.arange(half) + 0.5)[:, None] * positions[None, :]
    return np.concatenate([np.cos(angle), -np.sin(angle)], 0)


def make_tables():
    one = odd_tables(HALF_ONE, np.arange(2 * HALF_ONE))
    two = odd_tables(HALF_TWO, np.arange(ROWS))
    turn = np.zeros((HALF_ONE, LANES), np.float32)
    base = (2.0 * math.pi / (2 * HALF_ONE)) * (np.arange(HALF_ONE) + 0.5)
    turn[:, 0] = np.cos(base)
    turn[:, 1] = np.cos(2 * base)
    turn[:, 2] = -np.sin(base)
    turn[:, 3] = -np.sin(2 * base)
    return (
        split_np(one),
        split_np(one[:, TAPS:].T.copy()),
        split_np(two),
        split_np(two.T.copy()),
        turn,
    )


def split(value):
    high = value.astype(BF)
    return high, (value - high.astype(F32)).astype(BF)


def mm(left, right):
    return jnp.dot(left, right, preferred_element_type=F32)


def kernel(
    dims,
    query,
    key,
    value,
    short_taps,
    medium_taps,
    residues,
    decay_rates,
    skip_gain,
    norm_gain,
    fwd_one,
    inv_one,
    fwd_two,
    inv_two,
    turn,
    out,
    key_own,
    key_halo,
    value_own,
    value_halo,
    query_own,
    query_halo,
    staged,
    value_tilde,
    query_tilde,
    tap_spec,
    key_spec,
    kernel_spec,
    long_kernel,
    powers,
    eighth,
    mixed,
    states_own,
    states_away,
    states_seen,
    chip_state,
    chips_seen,
    row_state,
    rows_seen,
    carry_own,
    carry_away,
    carry_seen,
    local_long,
    gated,
    squares,
    row_sums,
    sums_seen,
    result,
    load_sems,
    send_sems,
    recv_sems,
    store_sem,
):
    n_x, n_y, n_z, channels = dims
    half = channels // 2
    seq = lax.axis_index("seq")
    chan = lax.axis_index("chan")
    core = seq % 2
    y_pos = (seq // 2) % n_y
    x_pos = seq // (2 * n_y)
    n_seq = 2 * n_x * n_y
    right = (seq + 1) % n_seq
    left = (seq + n_seq - 1) % n_seq
    other = seq + 1 - 2 * core

    def along_y(step):
        return (x_pos * n_y + (y_pos + step) % n_y) * 2 + core

    def along_x(step):
        return (((x_pos + step) % n_x) * n_y + y_pos) * 2 + core

    loads = [
        pltpu.make_async_copy(source, target, load_sems.at[number])
        for number, (source, target) in enumerate(
            ((key, key_own), (value, value_own), (query, query_own))
        )
    ]
    for load in loads:
        load.start()

    barrier = pltpu.get_barrier_semaphore()
    seq_partners = [right, left, other]
    seq_partners += [along_y(step) for step in range(1, n_y)]
    seq_partners += [along_x(step) for step in range(1, n_x)]
    for partner in seq_partners:
        pl.semaphore_signal(barrier, inc=1, device_id={"seq": partner}, device_id_type=MESH)
    for step in range(1, n_z):
        pl.semaphore_signal(
            barrier, inc=1, device_id={"chan": (chan + step) % n_z}, device_id_type=MESH
        )
    pl.semaphore_wait(barrier, len(seq_partners) + n_z - 1)

    sent = []

    def send(source, target, where):
        number = len(sent)
        copy = pltpu.make_async_remote_copy(
            src_ref=source,
            dst_ref=target,
            send_sem=send_sems.at[number],
            recv_sem=recv_sems.at[number],
            device_id=where,
            device_id_type=MESH,
        )
        copy.start()
        sent.append(copy)
        return copy

    key_copy = send(key.at[pl.ds(ROWS - TAPS - EDGE, TAPS + EDGE), :], key_halo, {"seq": right})
    value_copy = send(value.at[pl.ds(ROWS - EDGE, EDGE), :], value_halo, {"seq": right})
    query_copy = send(query.at[pl.ds(ROWS - EDGE, EDGE), :], query_halo, {"seq": right})

    def lanes(start, size):
        return pl.ds(pl.multiple_of(start, size), size)

    sub = lax.broadcasted_iota(jnp.int32, (8, LANES), 0).astype(F32)

    def pole_powers(group, _):
        cols = lanes(group * LANES, LANES)
        start = []
        steps = []
        for pole in range(POLES):
            rate = decay_rates[pl.ds(pole, 1), cols]
            power = jnp.exp(-rate * sub)
            powers[pole, :, cols] = power
            step = jnp.broadcast_to(jnp.exp(-8.0 * rate), (8, LANES))
            eighth[pole, :, cols] = step
            start.append(residues[pl.ds(pole, 1), cols] * power)
            steps.append(step)

        def rows(number, running):
            total = functools.reduce(jnp.add, running)
            long_kernel[pl.ds(pl.multiple_of(number * 8, 8), 8), cols] = total
            return tuple(r * s for r, s in zip(running, steps))

        lax.fori_loop(0, ROWS // 8, rows, tuple(start), unroll=4)
        return 0

    lax.fori_loop(0, channels // LANES, pole_powers, 0)

    loads[0].wait()

    def before_halo(tile, _):
        cols = lanes(tile * TILE, TILE)
        taps = medium_taps[:, cols]
        spec = mm(fwd_one[0, :, :TAPS], taps) + mm(fwd_one[1, :, :TAPS], taps)
        first = short_taps[1, :, cols].astype(F32)
        s_re = first[0:1] + first[1:2] * turn[:, 0:1] + first[2:3] * turn[:, 1:2]
        s_im = first[1:2] * turn[:, 2:3] + first[2:3] * turn[:, 3:4]
        m_re, m_im = spec[:HALF_ONE], spec[HALF_ONE:]
        scale = 1.0 / HALF_ONE
        tap_spec[:HALF_ONE, cols] = (m_re * s_re - m_im * s_im) * scale
        tap_spec[HALF_ONE:, cols] = (m_re * s_im + m_im * s_re) * scale
        own = key_own[:, cols]
        key_spec[:, cols] = mm(fwd_one[0, :, TAPS:], own) + mm(fwd_one[1, :, TAPS:], own)
        high, low = split(long_kernel[:, cols])
        spec = mm(fwd_two[0], high) + mm(fwd_two[0], low) + mm(fwd_two[1], high)
        kernel_spec[:, cols] = spec * (1.0 / HALF_TWO)
        return 0

    lax.fori_loop(0, channels // TILE, before_halo, 0)

    def short_conv(source, halo, taps_row, target):
        def one(tile, _):
            cols = lanes(tile * TILE, TILE)
            staged[0:EDGE, :] = halo[:, cols].astype(F32)
            staged[EDGE:, :] = source[:, cols].astype(F32)
            weights = short_taps[taps_row, :, cols].astype(F32)
            total = (
                weights[0:1] * staged[EDGE:, :]
                + weights[1:2] * staged[EDGE - 1 : EDGE - 1 + ROWS, :]
                + weights[2:3] * staged[EDGE - 2 : EDGE - 2 + ROWS, :]
            )
            target[:, cols] = total.astype(BF)
            return 0

        lax.fori_loop(0, channels // TILE, one, 0)

    loads[1].wait()
    loads[2].wait()
    key_copy.wait_recv()
    value_copy.wait_recv()
    query_copy.wait_recv()

    @pl.when(seq == 0)
    def _():
        key_halo[...] = jnp.zeros_like(key_halo)
        value_halo[...] = jnp.zeros_like(value_halo)
        query_halo[...] = jnp.zeros_like(query_halo)

    short_conv(value_own, value_halo, 2, value_tilde)

    def medium(tile, away):
        cols = lanes(tile * TILE, TILE)
        past = key_halo[EDGE:, cols]
        spec = key_spec[:, cols] + mm(fwd_one[0, :, :TAPS], past) + mm(fwd_one[1, :, :TAPS], past)
        x_re, x_im = spec[:HALF_ONE], spec[HALF_ONE:]
        t_re, t_im = tap_spec[:HALF_ONE, cols], tap_spec[HALF_ONE:, cols]
        re_high, re_low = split(x_re * t_re - x_im * t_im)
        im_high, im_low = split(x_re * t_im + x_im * t_re)
        high = jnp.concatenate([re_high, im_high], 0)
        low = jnp.concatenate([re_low, im_low], 0)
        key_hat = mm(inv_one[0], high) + mm(inv_one[0], low) + mm(inv_one[1], high)
        last = short_taps[1, 2:3, cols].astype(F32) * medium_taps[TAPS - EDGE :, cols].astype(F32)[
            EDGE - 1 :
        ]
        ends = (
            key_halo[:EDGE, cols].astype(F32)[EDGE - 1 :]
            + key_own[ROWS - EDGE :, cols].astype(F32)[EDGE - 1 :]
        )
        row = lax.broadcasted_iota(jnp.int32, (ROWS, TILE), 0)
        key_hat = key_hat + jnp.where(row == 0, last * ends, 0.0)
        mixed[:, cols] = (key_hat * value_tilde[:, cols].astype(F32)).astype(BF)

    def end_states(group, target, target_group):
        cols = lanes(group * LANES, LANES)
        steps = [eighth[pole, :, cols] for pole in range(POLES)]

        def rows(number, running):
            block = mixed[pl.ds(pl.multiple_of(number * 16, 16), 16), cols].astype(F32)
            running = [r * s + block[:8] for r, s in zip(running, steps)]
            return tuple(r * s + block[8:] for r, s in zip(running, steps))

        empty = tuple(jnp.zeros((8, LANES), F32) for _ in range(POLES))
        running = lax.fori_loop(0, ROWS // 16, rows, empty, unroll=2)
        to = lanes(target_group * LANES, LANES)
        for pole in range(POLES):
            rate = decay_rates[pl.ds(pole, 1), cols]
            weighted = running[pole] * jnp.exp(-rate * (7.0 - sub))
            target[pl.ds(pole, 1), to] = jnp.sum(weighted, axis=0, keepdims=True)

    half_tiles = half // TILE
    half_groups = half // LANES

    def half_block(side, target):
        lax.fori_loop(0, half_tiles, lambda n, _: (medium(side * half_tiles + n, 0), 0)[1], 0)
        lax.fori_loop(
            0,
            half_groups,
            lambda n, _: (end_states(side * half_groups + n, target, n), 0)[1],
            0,
        )

    half_block(1 - core, states_away)
    states_copy = send(states_away, states_seen, {"seq": other})
    half_block(core, states_own)

    own_cols = lanes(core * half, half)
    rates = decay_rates[:, own_cols]
    block_decay = jnp.exp(-float(ROWS) * rates)
    states_copy.wait_recv()
    mine, theirs = states_own[...], states_seen[...]
    first = jnp.where(core == 0, mine, theirs)
    second = jnp.where(core == 0, theirs, mine)
    chip_state[...] = block_decay * first + second
    y_copies = [
        send(chip_state, chips_seen.at[step - 1], {"seq": along_y(step)}) for step in range(1, n_y)
    ]

    def long_local(tile, _):
        cols = lanes(tile * TILE, TILE)
        signal = mixed[:, cols]
        spec = mm(fwd_two[0], signal) + mm(fwd_two[1], signal)
        x_re, x_im = spec[:HALF_TWO], spec[HALF_TWO:]
        k_re, k_im = kernel_spec[:HALF_TWO, cols], kernel_spec[HALF_TWO:, cols]
        re_high, re_low = split(x_re * k_re - x_im * k_im)
        im_high, im_low = split(x_re * k_im + x_im * k_re)
        high = jnp.concatenate([re_high, im_high], 0)
        low = jnp.concatenate([re_low, im_low], 0)
        local_long[:, cols] = mm(inv_two[0], high) + mm(inv_two[0], low) + mm(inv_two[1], high)
        return 0

    tiles = channels // TILE
    lax.fori_loop(0, tiles // 2, long_local, 0)

    chip_span = float(2 * ROWS)
    row_span = float(2 * ROWS * n_y)
    y_far = (n_y - 1 - y_pos).astype(F32)
    row_total = jnp.exp(-rates * (chip_span * y_far)) * chip_state[...]
    before = jnp.zeros((POLES, half), F32)
    for step in range(1, n_y):
        y_copies[step - 1].wait_recv()
        seen = chips_seen[step - 1]
        source = (y_pos - step + n_y) % n_y
        distance = (n_y - 1 - source).astype(F32)
        row_total += jnp.exp(-rates * (chip_span * distance)) * seen
        before += jnp.where(y_pos >= step, jnp.exp(-rates * (chip_span * (step - 1))) * seen, 0.0)
    row_state[...] = row_total
    x_copies = [
        send(row_state, rows_seen.at[step - 1], {"seq": along_x(step)}) for step in range(1, n_x)
    ]

    lax.fori_loop(tiles // 2, tiles, long_local, 0)

    above = jnp.zeros((POLES, half), F32)
    for step in range(1, n_x):
        x_copies[step - 1].wait_recv()
        above += jnp.where(
            x_pos >= step, jnp.exp(-rates * (row_span * (step - 1))) * rows_seen[step - 1], 0.0
        )
    before += jnp.exp(-rates * (chip_span * y_pos.astype(F32))) * above
    after = block_decay * before + first
    carry_own[...] = jnp.where(core == 0, before, after)
    carry_away[...] = jnp.where(core == 0, after, before)
    carry_copy = send(carry_away, carry_seen, {"seq": other})

    short_conv(query_own, query_halo, 0, query_tilde)
    squares[...] = jnp.zeros_like(squares)

    def gate(group, carry, carry_group):
        cols = lanes(group * LANES, LANES)
        of = lanes(carry_group * LANES, LANES)
        steps = [eighth[pole, :, cols] for pole in range(POLES)]
        start = []
        for pole in range(POLES):
            one = pl.ds(pole, 1)
            weight = residues[one, cols] * carry[one, of] * jnp.exp(-decay_rates[one, cols])
            start.append(weight * powers[pole, :, cols])
        skip = skip_gain[:, cols]

        def rows(number, running):
            top = functools.reduce(jnp.add, running)
            running = [r * s for r, s in zip(running, steps)]
            low = functools.reduce(jnp.add, running)
            running = tuple(r * s for r, s in zip(running, steps))
            at = pl.ds(pl.multiple_of(number * 16, 16), 16)
            long_out = local_long[at, cols] + jnp.concatenate([top, low], 0)
            long_out = long_out.astype(BF).astype(F32)
            total = query_tilde[at, cols].astype(F32) * (
                long_out + skip * mixed[at, cols].astype(F32)
            )
            gated[at, cols] = total
            squares[at, :] += total * total
            return running

        lax.fori_loop(0, ROWS // 16, rows, tuple(start), unroll=2)

    lax.fori_loop(
        0, half_groups, lambda n, _: (gate(core * half_groups + n, carry_own, n), 0)[1], 0
    )
    carry_copy.wait_recv()
    lax.fori_loop(
        0, half_groups, lambda n, _: (gate((1 - core) * half_groups + n, carry_seen, n), 0)[1], 0
    )

    row_sums[...] = jnp.sum(jnp.transpose(squares[...]), axis=0, keepdims=True)
    sum_copies = [
        send(row_sums, sums_seen.at[step - 1], {"chan": (chan + step) % n_z})
        for step in range(1, n_z)
    ]
    total = row_sums[...]
    for step in range(1, n_z):
        sum_copies[step - 1].wait_recv()
        total = total + sums_seen[step - 1]
    scale = lax.rsqrt(total * (1.0 / (channels * n_z)) + 1e-05)
    scale = jnp.transpose(jnp.broadcast_to(scale, (LANES, ROWS)))

    def finish(group, _):
        cols = lanes(group * LANES, LANES)
        result[:, cols] = (gated[:, cols] * scale * norm_gain[:, cols]).astype(BF)
        return 0

    lax.fori_loop(0, channels // LANES, finish, 0)
    store = pltpu.make_async_copy(result, out, store_sem)
    store.start()
    for copy in sent:
        copy.wait_send()
    store.wait()


def solution(mesh):
    n_seq, n_z = mesh.shape["seq"], mesh.shape["chan"]
    n_y = math.isqrt(n_seq // 2)
    n_x = n_seq // 2 // n_y
    tables = make_tables()

    def local(query, key, value, short_taps, medium_taps, residues, decay_rates, skip, gain):
        channels = query.shape[1]
        half = channels // 2
        n_copies = 3 + 1 + (n_y - 1) + (n_x - 1) + 1 + (n_z - 1)
        vmem = pltpu.VMEM
        scratch = [
            vmem((ROWS, channels), BF),
            vmem((TAPS + EDGE, channels), BF),
            vmem((ROWS, channels), BF),
            vmem((EDGE, channels), BF),
            vmem((ROWS, channels), BF),
            vmem((EDGE, channels), BF),
            vmem((EDGE + ROWS, TILE), F32),
            vmem((ROWS, channels), BF),
            vmem((ROWS, channels), BF),
            vmem((2 * HALF_ONE, channels), F32),
            vmem((2 * HALF_ONE, channels), F32),
            vmem((2 * HALF_TWO, channels), F32),
            vmem((ROWS, channels), F32),
            vmem((POLES, 8, channels), F32),
            vmem((POLES, 8, channels), F32),
            vmem((ROWS, channels), BF),
            vmem((POLES, half), F32),
            vmem((POLES, half), F32),
            vmem((POLES, half), F32),
            vmem((POLES, half), F32),
            vmem((n_y - 1, POLES, half), F32),
            vmem((POLES, half), F32),
            vmem((n_x - 1, POLES, half), F32),
            vmem((POLES, half), F32),
            vmem((POLES, half), F32),
            vmem((POLES, half), F32),
            vmem((ROWS, channels), F32),
            vmem((ROWS, channels), F32),
            vmem((ROWS, LANES), F32),
            vmem((1, ROWS), F32),
            vmem((n_z - 1, 1, ROWS), F32),
            vmem((ROWS, channels), BF),
            pltpu.SemaphoreType.DMA((3,)),
            pltpu.SemaphoreType.DMA((n_copies,)),
            pltpu.SemaphoreType.DMA((n_copies,)),
            pltpu.SemaphoreType.DMA,
        ]
        in_vmem = pl.BlockSpec(memory_space=pltpu.VMEM)
        anywhere = pl.BlockSpec(memory_space=pl.ANY)
        call = pl.pallas_call(
            functools.partial(kernel, (n_x, n_y, n_z, channels)),
            out_shape=jax.ShapeDtypeStruct((ROWS, channels), BF),
            in_specs=[anywhere] * 3 + [in_vmem] * 11,
            out_specs=anywhere,
            scratch_shapes=scratch,
            compiler_params=pltpu.CompilerParams(
                collective_id=0, has_side_effects=True, vmem_limit_bytes=48 * 1024 * 1024
            ),
        )
        return call(
            query,
            key,
            value,
            short_taps,
            medium_taps,
            residues,
            decay_rates,
            skip.reshape(1, channels),
            gain.reshape(1, channels),
            *tables,
        )

    in_specs = (
        P("seq", "chan"),
        P("seq", "chan"),
        P("seq", "chan"),
        P(None, None, "chan"),
        P(None, "chan"),
        P(None, "chan"),
        P(None, "chan"),
        P("chan"),
        P("chan"),
    )
    return jax.shard_map(
        local, mesh=mesh, in_specs=in_specs, out_specs=P("seq", "chan"), check_vma=False
    )
```

profile of v0, /device:TPU:1, one launch (start us, length us, event | category | flops | bytes accessed | tf_op | source)
XLA Modules:
  0.0 49.4 jit_solution(17388696622260900907)
XLA Ops:
  0.0 0.0 copy-start
  0.0 1.1 %copy-done = bf16[2,384,384]{2,1,0:T(8,128)(2,1)S(1)} copy-done((bf16[2,384,384]{2,1,0:T(8,128)(2,1)S(1)}, bf16[2,384,384]{2,1,0:T(8,128)(2,1)}, u32[]{:S(2)}) %copy-start) | copy-done | bytes 589848
  1.1 0.0 copy-start.1
  1.1 1.0 %copy-done.1 = bf16[256,1024]{1,0:T(8,128)(2,1)S(1)} copy-done((bf16[256,1024]{1,0:T(8,128)(2,1)S(1)}, bf16[256,1024]{1,0:T(8,128)(2,1)}, u32[]{:S(2)}) %copy-start.1) | copy-done | bytes 524312
  2.1 0.0 copy-start.2
  2.1 1.0 %copy-done.2 = bf16[256,1024]{1,0:T(8,128)(2,1)S(1)} copy-done((bf16[256,1024]{1,0:T(8,128)(2,1)S(1)}, bf16[256,1024]{1,0:T(8,128)(2,1)}, u32[]{:S(2)}) %copy-start.2) | copy-done | bytes 524312
  3.1 0.0 copy-start.3
  3.2 1.0 %copy-done.3 = bf16[256,1024]{1,0:T(8,128)(2,1)S(1)} copy-done((bf16[256,1024]{1,0:T(8,128)(2,1)S(1)}, bf16[256,1024]{1,0:T(8,128)(2,1)}, u32[]{:S(2)}) %copy-start.3) | copy-done | bytes 524312
  4.2 0.0 copy-start.4
  4.2 1.0 %copy-done.4 = bf16[2,256,512]{2,1,0:T(8,128)(2,1)S(1)} copy-done((bf16[2,256,512]{2,1,0:T(8,128)(2,1)S(1)}, bf16[2,256,512]{2,1,0:T(8,128)(2,1)}, u32[]{:S(2)}) %copy-start.4) | copy-done | bytes 524312
  5.2 0.0 copy-start.5
  5.2 1.0 %copy-done.5 = bf16[2,512,256]{2,1,0:T(8,128)(2,1)S(1)} copy-done((bf16[2,512,256]{2,1,0:T(8,128)(2,1)S(1)}, bf16[2,512,256]{2,1,0:T(8,128)(2,1)}, u32[]{:S(2)}) %copy-start.5) | copy-done | bytes 524312
  6.3 0.0 copy-start.6
  6.3 1.0 %copy-done.6 = bf16[2,256,384]{2,1,0:T(8,128)(2,1)S(1)} copy-done((bf16[2,256,384]{2,1,0:T(8,128)(2,1)S(1)}, bf16[2,256,384]{2,1,0:T(8,128)(2,1)}, u32[]{:S(2)}) %copy-start.6) | copy-done | bytes 393240
  7.3 0.0 copy-start.7
  7.3 0.9 %copy-done.7 = bf16[128,1024]{1,0:T(8,128)(2,1)S(1)} copy-done((bf16[128,1024]{1,0:T(8,128)(2,1)S(1)}, bf16[128,1024]{1,0:T(8,128)(2,1)}, u32[]{:S(2)}) %copy-start.7) | copy-done | bytes 262168
  8.2 0.0 copy-start.8
  8.2 0.9 %copy-done.8 = f32[192,128]{1,0:T(8,128)S(1)} copy-done((f32[192,128]{1,0:T(8,128)S(1)}, f32[192,128]{1,0:T(8,128)}, u32[]{:S(2)}) %copy-start.8) | copy-done | bytes 98328
  9.1 0.0 copy-start.9
  9.1 0.8 %copy-done.9 = f32[16,1024]{1,0:T(8,128)S(1)} copy-done((f32[16,1024]{1,0:T(8,128)S(1)}, f32[16,1024]{1,0:T(8,128)}, u32[]{:S(2)}) %copy-start.9) | copy-done | bytes 65560
  10.0 0.0 copy-start.10
  10.0 0.8 %copy-done.10 = f32[16,1024]{1,0:T(8,128)S(1)} copy-done((f32[16,1024]{1,0:T(8,128)S(1)}, f32[16,1024]{1,0:T(8,128)}, u32[]{:S(2)}) %copy-start.10) | copy-done | bytes 65560
  10.8 0.0 copy-start.11
  10.8 0.7 %copy-done.11 = bf16[3,3,1024]{2,1,0:T(4,128)(2,1)S(1)} copy-done((bf16[3,3,1024]{2,1,0:T(4,128)(2,1)S(1)}, bf16[3,3,1024]{2,1,0:T(4,128)(2,1)}, u32[]{:S(2)}) %copy-start.11) | copy-done | bytes 18456
  11.5 0.0 copy-start.12
  11.5 0.7 %copy-done.12 = f32[1024]{0:T(1024)S(1)} copy-done((f32[1024]{0:T(1024)S(1)}, f32[1024]{0:T(1024)}, u32[]{:S(2)}) %copy-start.12) | copy-done | bytes 4120
  12.2 0.0 copy-start.13
  12.2 0.7 %copy-done.13 = f32[1024]{0:T(1024)S(1)} copy-done((f32[1024]{0:T(1024)S(1)}, f32[1024]{0:T(1024)}, u32[]{:S(2)}) %copy-start.13) | copy-done | bytes 4120
  12.9 35.7 %shard_map.136 = bf16[256,1024]{1,0:T(8,128)(2,1)S(1)} custom-call(bf16[256,1024]{1,0:T(8,128)(2,1)S(1)} %copy-done.1, bf16[256,1024]{1,0:T(8,128)(2,1)S(1)} %copy-done.2, bf16[256,1024]{1,0:T(8,128)(2,1)S(1)} %copy-done.3, bf16[3,3,1024]{2,1,0:T(4,128)(2,1)S(1)} %copy-done.11, bf16[128,1024]{1,0:T(8,128)(2,1)S(1)} %copy-done.7, f32[16,1024]{1,0:T(8,128)S(1)} %copy-done.9, ...), custom_call_target="tpu_custom_call" | custom-call | tf_op jit(solution)/shard_map/pallas_call | solution.py:497
  48.6 0.8 %copy.16 = bf16[256,1024]{1,0:T(8,128)(2,1)} copy(bf16[256,1024]{1,0:T(8,128)(2,1)S(1)} %shard_map.136) | data formatting | bytes 1048576
Async XLA Ops:
  0.0 1.1 %copy-start = (bf16[2,384,384]{2,1,0:T(8,128)(2,1)S(1)}, bf16[2,384,384]{2,1,0:T(8,128)(2,1)}, u32[]{:S(2)}) copy-start(bf16[2,384,384]{2,1,0:T(8,128)(2,1)} %constant.10.clone.fwd_one) | copy-start | bytes 1769476
  1.1 1.0 %copy-start.1 = (bf16[256,1024]{1,0:T(8,128)(2,1)S(1)}, bf16[256,1024]{1,0:T(8,128)(2,1)}, u32[]{:S(2)}) copy-start(bf16[256,1024]{1,0:T(8,128)(2,1)} %query.1) | copy-start | bytes 1572868
  2.1 1.0 %copy-start.2 = (bf16[256,1024]{1,0:T(8,128)(2,1)S(1)}, bf16[256,1024]{1,0:T(8,128)(2,1)}, u32[]{:S(2)}) copy-start(bf16[256,1024]{1,0:T(8,128)(2,1)} %key.1) | copy-start | bytes 1572868
  3.1 1.0 %copy-start.3 = (bf16[256,1024]{1,0:T(8,128)(2,1)S(1)}, bf16[256,1024]{1,0:T(8,128)(2,1)}, u32[]{:S(2)}) copy-start(bf16[256,1024]{1,0:T(8,128)(2,1)} %value.1) | copy-start | bytes 1572868
  4.2 1.0 %copy-start.4 = (bf16[2,256,512]{2,1,0:T(8,128)(2,1)S(1)}, bf16[2,256,512]{2,1,0:T(8,128)(2,1)}, u32[]{:S(2)}) copy-start(bf16[2,256,512]{2,1,0:T(8,128)(2,1)} %constant.13.clone.inv_two) | copy-start | bytes 1572868
  5.2 1.0 %copy-start.5 = (bf16[2,512,256]{2,1,0:T(8,128)(2,1)S(1)}, bf16[2,512,256]{2,1,0:T(8,128)(2,1)}, u32[]{:S(2)}) copy-start(bf16[2,512,256]{2,1,0:T(8,128)(2,1)} %constant.12.clone.fwd_two) | copy-start | bytes 1572868
  6.3 1.0 %copy-start.6 = (bf16[2,256,384]{2,1,0:T(8,128)(2,1)S(1)}, bf16[2,256,384]{2,1,0:T(8,128)(2,1)}, u32[]{:S(2)}) copy-start(bf16[2,256,384]{2,1,0:T(8,128)(2,1)} %constant.11.clone.inv_one) | copy-start | bytes 1179652
  7.3 0.9 %copy-start.7 = (bf16[128,1024]{1,0:T(8,128)(2,1)S(1)}, bf16[128,1024]{1,0:T(8,128)(2,1)}, u32[]{:S(2)}) copy-start(bf16[128,1024]{1,0:T(8,128)(2,1)} %medium_taps.1) | copy-start | bytes 786436
  8.2 0.9 %copy-start.8 = (f32[192,128]{1,0:T(8,128)S(1)}, f32[192,128]{1,0:T(8,128)}, u32[]{:S(2)}) copy-start(f32[192,128]{1,0:T(8,128)} %constant.14.clone.turn) | copy-start | bytes 294916
  9.1 0.8 %copy-start.9 = (f32[16,1024]{1,0:T(8,128)S(1)}, f32[16,1024]{1,0:T(8,128)}, u32[]{:S(2)}) copy-start(f32[16,1024]{1,0:T(8,128)} %residues.1) | copy-start | bytes 196612
  10.0 0.8 %copy-start.10 = (f32[16,1024]{1,0:T(8,128)S(1)}, f32[16,1024]{1,0:T(8,128)}, u32[]{:S(2)}) copy-start(f32[16,1024]{1,0:T(8,128)} %decay_rates.1) | copy-start | bytes 196612
  10.8 0.7 %copy-start.11 = (bf16[3,3,1024]{2,1,0:T(4,128)(2,1)S(1)}, bf16[3,3,1024]{2,1,0:T(4,128)(2,1)}, u32[]{:S(2)}) copy-start(bf16[3,3,1024]{2,1,0:T(4,128)(2,1)} %short_taps.1) | copy-start | bytes 55300
  11.5 0.7 %copy-start.12 = (f32[1024]{0:T(1024)S(1)}, f32[1024]{0:T(1024)}, u32[]{:S(2)}) copy-start(f32[1024]{0:T(1024)} %param.21) | copy-start | bytes 12292
  12.2 0.7 %copy-start.13 = (f32[1024]{0:T(1024)S(1)}, f32[1024]{0:T(1024)}, u32[]{:S(2)}) copy-start(f32[1024]{0:T(1024)} %param.22) | copy-start | bytes 12292
where the time goes:
time: 50.1 us; the launch traced here: 49.4 us
  Pallas kernels  35.7 us (71%)
  local copies, waits for them, and re-layouts  13.7 us (27%)
    pallas_call x1, Pallas kernels, local(): call(query, key, value, short_taps, medium_taps, residues, decay_rates, s...  35.7 us
    unnamed x29, local copies, waits for them, and re-layouts  13.7 us

commit v1 on v0

--- a/solution.py
+++ b/solution.py
@@ -53,6 +53,10 @@
     )
 
 
+def run(name, task):
+    task()
+
+
 def split(value):
     high = value.astype(BF)
     return high, (value - high.astype(F32)).astype(BF)
@@ -67,18 +71,20 @@
     query,
     key,
     value,
-    short_taps,
-    medium_taps,
-    residues,
-    decay_rates,
-    skip_gain,
-    norm_gain,
-    fwd_one,
-    inv_one,
-    fwd_two,
-    inv_two,
-    turn,
+    *rest,
+):
+    sources, out, buffers, scratch = rest[:11], rest[11], rest[12:23], rest[23:]
+    body(dims, query, key, value, sources, out, buffers, *scratch)
+
+
+def body(
+    dims,
+    query,
+    key,
+    value,
+    sources,
     out,
+    buffers,
     key_own,
     key_halo,
     value_own,
@@ -110,13 +116,24 @@
     squares,
     row_sums,
     sums_seen,
-    result,
     load_sems,
     send_sems,
     recv_sems,
-    store_sem,
 ):
     n_x, n_y, n_z, channels = dims
+    (
+        short_taps,
+        medium_taps,
+        residues,
+        decay_rates,
+        skip_gain,
+        norm_gain,
+        fwd_one,
+        inv_one,
+        fwd_two,
+        inv_two,
+        turn,
+    ) = buffers
     half = channels // 2
     seq = lax.axis_index("seq")
     chan = lax.axis_index("chan")
@@ -134,11 +151,13 @@
     def along_x(step):
         return (((x_pos + step) % n_x) * n_y + y_pos) * 2 + core
 
+    order = (3, 2, 10, 6, 1, 0, 8, 7, 9, 4, 5)
+    pairs = [(sources[n], buffers[n]) for n in order[:2]] + [(key, key_own)]
+    pairs += [(sources[n], buffers[n]) for n in order[2:]]
+    pairs += [(value, value_own), (query, query_own)]
     loads = [
         pltpu.make_async_copy(source, target, load_sems.at[number])
-        for number, (source, target) in enumerate(
-            ((key, key_own), (value, value_own), (query, query_own))
-        )
+        for number, (source, target) in enumerate(pairs)
     ]
     for load in loads:
         load.start()
@@ -178,6 +197,9 @@
     def lanes(start, size):
         return pl.ds(pl.multiple_of(start, size), size)
 
+    loads[0].wait()
+    loads[1].wait()
+
     sub = lax.broadcasted_iota(jnp.int32, (8, LANES), 0).astype(F32)
 
     def pole_powers(group, _):
@@ -201,9 +223,10 @@
         lax.fori_loop(0, ROWS // 8, rows, tuple(start), unroll=4)
         return 0
 
-    lax.fori_loop(0, channels // LANES, pole_powers, 0)
-
-    loads[0].wait()
+    run("powers", lambda: lax.fori_loop(0, channels // LANES, pole_powers, 0))
+
+    for load in loads[2:8]:
+        load.wait()
 
     def before_halo(tile, _):
         cols = lanes(tile * TILE, TILE)
@@ -223,7 +246,7 @@
         kernel_spec[:, cols] = spec * (1.0 / HALF_TWO)
         return 0
 
-    lax.fori_loop(0, channels // TILE, before_halo, 0)
+    run("before", lambda: lax.fori_loop(0, channels // TILE, before_halo, 0))
 
     def short_conv(source, halo, taps_row, target):
         def one(tile, _):
@@ -241,8 +264,8 @@
 
         lax.fori_loop(0, channels // TILE, one, 0)
 
-    loads[1].wait()
-    loads[2].wait()
+    for load in loads[8:]:
+        load.wait()
     key_copy.wait_recv()
     value_copy.wait_recv()
     query_copy.wait_recv()
@@ -253,9 +276,9 @@
         value_halo[...] = jnp.zeros_like(value_halo)
         query_halo[...] = jnp.zeros_like(query_halo)
 
-    short_conv(value_own, value_halo, 2, value_tilde)
-
-    def medium(tile, away):
+    run("value", lambda: short_conv(value_own, value_halo, 2, value_tilde))
+
+    def medium(tile):
         cols = lanes(tile * TILE, TILE)
         past = key_halo[EDGE:, cols]
         spec = key_spec[:, cols] + mm(fwd_one[0, :, :TAPS], past) + mm(fwd_one[1, :, :TAPS], past)
@@ -298,13 +321,16 @@
     half_groups = half // LANES
 
     def half_block(side, target):
-        lax.fori_loop(0, half_tiles, lambda n, _: (medium(side * half_tiles + n, 0), 0)[1], 0)
-        lax.fori_loop(
-            0,
-            half_groups,
-            lambda n, _: (end_states(side * half_groups + n, target, n), 0)[1],
-            0,
-        )
+        def medium_tile(n, _):
+            medium(side * half_tiles + n)
+            return 0
+
+        def state_group(n, _):
+            end_states(side * half_groups + n, target, n)
+            return 0
+
+        run("medium", lambda: lax.fori_loop(0, half_tiles, medium_tile, 0))
+        run("states", lambda: lax.fori_loop(0, half_groups, state_group, 0))
 
     half_block(1 - core, states_away)
     states_copy = send(states_away, states_seen, {"seq": other})
@@ -336,7 +362,7 @@
         return 0
 
     tiles = channels // TILE
-    lax.fori_loop(0, tiles // 2, long_local, 0)
+    run("long1", lambda: lax.fori_loop(0, tiles // 2, long_local, 0))
 
     chip_span = float(2 * ROWS)
     row_span = float(2 * ROWS * n_y)
@@ -355,7 +381,7 @@
         send(row_state, rows_seen.at[step - 1], {"seq": along_x(step)}) for step in range(1, n_x)
     ]
 
-    lax.fori_loop(tiles // 2, tiles, long_local, 0)
+    run("long2", lambda: lax.fori_loop(tiles // 2, tiles, long_local, 0))
 
     above = jnp.zeros((POLES, half), F32)
     for step in range(1, n_x):
@@ -369,7 +395,7 @@
     carry_away[...] = jnp.where(core == 0, after, before)
     carry_copy = send(carry_away, carry_seen, {"seq": other})
 
-    short_conv(query_own, query_halo, 0, query_tilde)
+    run("query", lambda: short_conv(query_own, query_halo, 0, query_tilde))
     squares[...] = jnp.zeros_like(squares)
 
     def gate(group, carry, carry_group):
@@ -400,13 +426,16 @@
 
         lax.fori_loop(0, ROWS // 16, rows, tuple(start), unroll=2)
 
-    lax.fori_loop(
-        0, half_groups, lambda n, _: (gate(core * half_groups + n, carry_own, n), 0)[1], 0
-    )
+    def gate_half(side, carry):
+        def one(n, _):
+            gate(side * half_groups + n, carry, n)
+            return 0
+
+        run("gate", lambda: lax.fori_loop(0, half_groups, one, 0))
+
+    gate_half(core, carry_own)
     carry_copy.wait_recv()
-    lax.fori_loop(
-        0, half_groups, lambda n, _: (gate((1 - core) * half_groups + n, carry_seen, n), 0)[1], 0
-    )
+    gate_half(1 - core, carry_seen)
 
     row_sums[...] = jnp.sum(jnp.transpose(squares[...]), axis=0, keepdims=True)
     sum_copies = [
@@ -422,15 +451,12 @@
 
     def finish(group, _):
         cols = lanes(group * LANES, LANES)
-        result[:, cols] = (gated[:, cols] * scale * norm_gain[:, cols]).astype(BF)
+        out[:, cols] = (gated[:, cols] * scale * norm_gain[:, cols]).astype(BF)
         return 0
 
-    lax.fori_loop(0, channels // LANES, finish, 0)
-    store = pltpu.make_async_copy(result, out, store_sem)
-    store.start()
+    run("finish", lambda: lax.fori_loop(0, channels // LANES, finish, 0))
     for copy in sent:
         copy.wait_send()
-    store.wait()
 
 
 def solution(mesh):
@@ -442,6 +468,18 @@
     def local(query, key, value, short_taps, medium_taps, residues, decay_rates, skip, gain):
         channels = query.shape[1]
         half = channels // 2
+        operands = (
+            query,
+            key,
+            value,
+            short_taps,
+            medium_taps,
+            residues,
+            decay_rates,
+            skip.reshape(1, channels),
+            gain.reshape(1, channels),
+            *(jnp.asarray(table) for table in tables),
+        )
         n_copies = 3 + 1 + (n_y - 1) + (n_x - 1) + 1 + (n_z - 1)
         vmem = pltpu.VMEM
         scratch = [
@@ -476,36 +514,22 @@
             vmem((ROWS, LANES), F32),
             vmem((1, ROWS), F32),
             vmem((n_z - 1, 1, ROWS), F32),
-            vmem((ROWS, channels), BF),
-            pltpu.SemaphoreType.DMA((3,)),
+            pltpu.SemaphoreType.DMA((len(operands),)),
             pltpu.SemaphoreType.DMA((n_copies,)),
             pltpu.SemaphoreType.DMA((n_copies,)),
-            pltpu.SemaphoreType.DMA,
         ]
-        in_vmem = pl.BlockSpec(memory_space=pltpu.VMEM)
-        anywhere = pl.BlockSpec(memory_space=pl.ANY)
+        in_hbm = pl.BlockSpec(memory_space=pltpu.HBM)
         call = pl.pallas_call(
             functools.partial(kernel, (n_x, n_y, n_z, channels)),
             out_shape=jax.ShapeDtypeStruct((ROWS, channels), BF),
-            in_specs=[anywhere] * 3 + [in_vmem] * 11,
-            out_specs=anywhere,
-            scratch_shapes=scratch,
+            in_specs=[in_hbm] * len(operands),
+            out_specs=pl.BlockSpec(memory_space=pltpu.VMEM),
+            scratch_shapes=[vmem(x.shape, x.dtype) for x in operands[3:]] + scratch,
             compiler_params=pltpu.CompilerParams(
-                collective_id=0, has_side_effects=True, vmem_limit_bytes=48 * 1024 * 1024
+                collective_id=0, has_side_effects=True, vmem_limit_bytes=60 * 1024 * 1024
             ),
         )
-        return call(
-            query,
-            key,
-            value,
-            short_taps,
-            medium_taps,
-            residues,
-            decay_rates,
-            skip.reshape(1, channels),
-            gain.reshape(1, channels),
-            *tables,
-        )
+        return call(*operands)
 
     in_specs = (
         P("seq", "chan"),

time: 50.1 us -> 38.7 us (0.77); the launches traced: 49.4 us -> 38.5 us
  local copies, waits for them, and re-layouts: 13.7 us -> 1.87 us
  Pallas kernels: 35.7 us -> 36.7 us
    unnamed x29 -> x1, local copies, waits for them, and re-layouts: 13.7 us -> 1.87 us
    pallas_call x1, Pallas kernels: 35.7 us -> 36.7 us  [local(): return call(*operands)]
where the time goes in v1:
time: 38.7 us; the launch traced here: 38.5 us
  Pallas kernels  36.7 us (95%)
  local copies, waits for them, and re-layouts  1.87 us (5%)
    pallas_call x1, Pallas kernels, local(): return call(*operands)  36.7 us
    unnamed x1, local copies, waits for them, and re-layouts  1.87 us

profile of v1, /device:TPU:1, one launch (start us, length us, event | category | flops | bytes accessed | tf_op | source)
XLA Modules:
  0.0 38.5 jit_solution(14780957634683743570)
XLA Ops:
  0.0 36.7 %shard_map.136 = bf16[256,1024]{1,0:T(8,128)(2,1)} custom-call(bf16[256,1024]{1,0:T(8,128)(2,1)} %query.1, bf16[256,1024]{1,0:T(8,128)(2,1)} %key.1, bf16[256,1024]{1,0:T(8,128)(2,1)} %value.1, bf16[3,3,1024]{2,1,0:T(4,128)(2,1)} %rest_0_.1, bf16[128,1024]{1,0:T(8,128)(2,1)} %rest_1_.1, f32[16,1024]{1,0:T(8,128)} %rest_2_.1, f32[16,1024]{1,0:T(8,128)} %rest_3_.1, ...), custom_call_target="tpu_custom_call" | custom-call | tf_op jit(solution)/shard_map/pallas_call | solution.py:532
  36.7 1.9 %copy.16 = bf16[256,1024]{1,0:T(8,128)(2,1)} copy(bf16[256,1024]{1,0:T(8,128)(2,1)} %shard_map.136) | data formatting | bytes 1048576

commit v2 on v1

v2 whole, which is shorter than its diff:
```python
import functools
import math

import jax
import jax.numpy as jnp
import ml_dtypes
import numpy as np
from jax import lax
from jax.experimental import pallas as pl
from jax.experimental.pallas import tpu as pltpu
from jax.sharding import PartitionSpec as P

D = 8192
ROWS = 256
TAPS = 128
POLES = 16
LANES = 128
TILE = 256
EDGE = 16
HALF_ONE = 192
HALF_TWO = 256
MESH = pl.DeviceIdType.MESH
BF = jnp.bfloat16
F32 = jnp.float32


def narrow(table):
    return np.ascontiguousarray(table).astype(np.float32).astype(ml_dtypes.bfloat16)


def odd_tables(half, positions):
    angle = (2.0 * math.pi / (2 * half)) * (np.arange(half) + 0.5)[:, None] * positions[None, :]
    return np.concatenate([np.cos(angle), -np.sin(angle)], 0)


def make_tables():
    one = odd_tables(HALF_ONE, np.arange(2 * HALF_ONE))
    two = odd_tables(HALF_TWO, np.arange(ROWS))
    turn = np.zeros((HALF_ONE, LANES), np.float32)
    base = (2.0 * math.pi / (2 * HALF_ONE)) * (np.arange(HALF_ONE) + 0.5)
    turn[:, 0] = np.cos(base)
    turn[:, 1] = np.cos(2 * base)
    turn[:, 2] = -np.sin(base)
    turn[:, 3] = -np.sin(2 * base)
    return (
        narrow(one),
        narrow(one[:, TAPS:].T),
        narrow(two),
        narrow(two.T),
        turn,
    )


def run(name, task):
    task()


def split(value):
    high = value.astype(BF)
    return high, (value - high.astype(F32)).astype(BF)


def mm(left, right):
    return jnp.dot(left, right, preferred_element_type=F32)


def kernel(
    dims,
    query,
    key,
    value,
    *rest,
):
    sources, out, buffers, scratch = rest[:11], rest[11], rest[12:23], rest[23:]
    body(dims, query, key, value, sources, out, buffers, *scratch)


def body(
    dims,
    query,
    key,
    value,
    sources,
    out,
    buffers,
    key_own,
    key_halo,
    value_own,
    value_halo,
    query_own,
    query_halo,
    staged,
    value_tilde,
    query_tilde,
    tap_spec,
    key_spec,
    kernel_spec,
    long_kernel,
    powers,
    eighth,
    mixed,
    states_own,
    states_away,
    states_seen,
    chip_state,
    chips_seen,
    row_state,
    rows_seen,
    carry_own,
    carry_away,
    carry_seen,
    local_long,
    gated,
    squares,
    row_sums,
    sums_seen,
    load_sems,
    send_sems,
    recv_sems,
    y_relay,
    x_relay,
    z_relay,
):
    n_x, n_y, n_z, channels = dims
    (
        short_taps,
        medium_taps,
        residues,
        decay_rates,
        skip_gain,
        norm_gain,
        fwd_one,
        inv_one,
        fwd_two,
        inv_two,
        turn,
    ) = buffers
    half = channels // 2
    seq = lax.axis_index("seq")
    chan = lax.axis_index("chan")
    core = seq % 2
    y_pos = (seq // 2) % n_y
    x_pos = seq // (2 * n_y)
    n_seq = 2 * n_x * n_y
    right = (seq + 1) % n_seq
    left = (seq + n_seq - 1) % n_seq
    other = seq + 1 - 2 * core

    def along_y(step):
        return (x_pos * n_y + (y_pos + step) % n_y) * 2 + core

    def along_z(step):
        return {"chan": (chan + step) % n_z}

    def lanes(start, size):
        return pl.ds(pl.multiple_of(start, size), size)

    def along_x(step):
        return (((x_pos + step) % n_x) * n_y + y_pos) * 2 + core

    pairs = [(sources[n], buffers[n]) for n in (3, 6, 1, 0, 10)] + [(key, key_own)]
    pairs += [(value, value_own)] + [(sources[n], buffers[n]) for n in (2, 7, 8, 9, 4, 5)]
    pairs += [(query, query_own)]
    loads = [
        pltpu.make_async_copy(source, target, load_sems.at[number])
        for number, (source, target) in enumerate(pairs)
    ]
    for load in loads:
        load.start()

    barrier = pltpu.get_barrier_semaphore()
    near = [{"seq": right}, {"seq": left}, {"seq": other}]
    near += [{"seq": along_y(1)}, {"seq": along_y(n_y - 1)}]
    near += [{"seq": along_x(1)}, {"seq": along_x(n_x - 1)}]
    near += [along_z(1), along_z(n_z - 1)]
    for partner in near:
        pl.semaphore_signal(barrier, inc=1, device_id=partner, device_id_type=MESH)

    sub = lax.broadcasted_iota(jnp.int32, (8, LANES), 0).astype(F32)
    loads[0].wait()

    def pole_powers(group, _):
        cols = lanes(group * LANES, LANES)
        for pole in range(POLES):
            rate = decay_rates[pl.ds(pole, 1), cols]
            powers[pole, :, cols] = jnp.exp(-rate * sub)
            eighth[pole, :, cols] = jnp.broadcast_to(jnp.exp(-8.0 * rate), (8, LANES))
        return 0

    run("powers", lambda: lax.fori_loop(0, channels // LANES, pole_powers, 0))
    pl.semaphore_wait(barrier, len(near))

    def relay(sems, along, size, step):
        for way, sign in enumerate((1, size - 1)):
            pl.semaphore_signal(
                sems.at[step - 2, way], inc=1, device_id=along(sign), device_id_type=MESH
            )

    def relayed(sems, step):
        for way in range(2):
            pl.semaphore_wait(sems.at[step - 2, way], 1)

    def seq_y(step):
        return {"seq": along_y(step)}

    def seq_x(step):
        return {"seq": along_x(step)}

    for step in range(2, n_y // 2 + 1):
        relay(y_relay, seq_y, n_y, step)
        relayed(y_relay, step) if step < n_y // 2 else None
    for step in range(2, n_x // 2 + 1):
        relay(x_relay, seq_x, n_x, step)
        relayed(x_relay, step) if step < n_x // 2 else None
    if n_z > 3:
        relay(z_relay, along_z, n_z, 2)

    sent = []

    def send(source, target, where):
        number = len(sent)
        copy = pltpu.make_async_remote_copy(
            src_ref=source,
            dst_ref=target,
            send_sem=send_sems.at[number],
            recv_sem=recv_sems.at[number],
            device_id=where,
            device_id_type=MESH,
        )
        copy.start()
        sent.append(copy)
        return copy

    tiles = channels // TILE
    half_tiles = half // TILE
    half_groups = half // LANES

    def chunk(side, number):
        return (side if number < half_tiles else 1 - side) * half_tiles + number % half_tiles

    key_copies = []
    for number in range(tiles):
        piece = key.at[
            pl.ds(ROWS - TAPS - EDGE, TAPS + EDGE), lanes(chunk(core, number) * TILE, TILE)
        ]
        key_copies.append(send(piece, key_halo.at[number], {"seq": right}))
        if number == 0:
            value_copy = send(value.at[pl.ds(ROWS - EDGE, EDGE), :], value_halo, {"seq": right})
    query_copy = send(query.at[pl.ds(ROWS - EDGE, EDGE), :], query_halo, {"seq": right})

    for load in loads[1:6]:
        load.wait()

    def before_halo(tile, _):
        cols = lanes(tile * TILE, TILE)
        taps = medium_taps[:, cols]
        spec = mm(fwd_one[:, :TAPS], taps)
        first = short_taps[1, :, cols].astype(F32)
        s_re = first[0:1] + first[1:2] * turn[:, 0:1] + first[2:3] * turn[:, 1:2]
        s_im = first[1:2] * turn[:, 2:3] + first[2:3] * turn[:, 3:4]
        m_re, m_im = spec[:HALF_ONE], spec[HALF_ONE:]
        scale = 1.0 / HALF_ONE
        tap_spec[:HALF_ONE, cols] = (m_re * s_re - m_im * s_im) * scale
        tap_spec[HALF_ONE:, cols] = (m_re * s_im + m_im * s_re) * scale
        key_spec[:, cols] = mm(fwd_one[:, TAPS:], key_own[:, cols])
        return 0

    run("before", lambda: lax.fori_loop(0, channels // TILE, before_halo, 0))

    def short_conv(source, halo, taps_row, target, count):
        def one(tile, _):
            cols = lanes(tile * TILE, TILE)
            if halo is None:
                staged[0:EDGE, :] = jnp.zeros((EDGE, TILE), F32)
            else:
                staged[0:EDGE, :] = halo[:, cols].astype(F32)
            staged[EDGE : EDGE + count, :] = source[0:count, cols].astype(F32)
            weights = short_taps[taps_row, :, cols].astype(F32)
            total = (
                weights[0:1] * staged[EDGE : EDGE + count, :]
                + weights[1:2] * staged[EDGE - 1 : EDGE - 1 + count, :]
                + weights[2:3] * staged[EDGE - 2 : EDGE - 2 + count, :]
            )
            target[0:count, cols] = total.astype(BF)
            return 0

        lax.fori_loop(0, tiles, one, 0)

    for load in loads[6:8]:
        load.wait()
    run("value", lambda: short_conv(value_own, None, 2, value_tilde, ROWS))

    def pole_kernel(group, _):
        cols = lanes(group * LANES, LANES)
        steps = [eighth[pole, :, cols] for pole in range(POLES)]
        start = [residues[pl.ds(pole, 1), cols] * powers[pole, :, cols] for pole in range(POLES)]

        def rows(number, running):
            total = functools.reduce(jnp.add, running)
            long_kernel[pl.ds(pl.multiple_of(number * 8, 8), 8), cols] = total
            return tuple(r * s for r, s in zip(running, steps))

        lax.fori_loop(0, ROWS // 8, rows, tuple(start), unroll=4)
        return 0

    run("kernel", lambda: lax.fori_loop(0, channels // LANES, pole_kernel, 0))

    for load in loads[8:]:
        load.wait()

    def medium(number, tile):
        cols = lanes(tile * TILE, TILE)
        spec = key_spec[:, cols] + mm(fwd_one[:, :TAPS], key_halo[number, EDGE:])
        x_re, x_im = spec[:HALF_ONE], spec[HALF_ONE:]
        t_re, t_im = tap_spec[:HALF_ONE, cols], tap_spec[HALF_ONE:, cols]
        re, im = x_re * t_re - x_im * t_im, x_re * t_im + x_im * t_re
        key_hat = mm(inv_one[...], jnp.concatenate([re.astype(BF), im.astype(BF)], 0))
        last = short_taps[1, 2:3, cols].astype(F32) * medium_taps[TAPS - EDGE :, cols].astype(F32)[
            EDGE - 1 :
        ]
        ends = (
            key_halo[number, :EDGE].astype(F32)[EDGE - 1 :]
            + key_own[ROWS - EDGE :, cols].astype(F32)[EDGE - 1 :]
        )
        row = lax.broadcasted_iota(jnp.int32, (ROWS, TILE), 0)
        key_hat = key_hat + jnp.where(row == 0, last * ends, 0.0)
        mixed[:, cols] = (key_hat * value_tilde[:, cols].astype(F32)).astype(BF)

    def end_states(group, target, target_group):
        cols = lanes(group * LANES, LANES)
        steps = [eighth[pole, :, cols] for pole in range(POLES)]

        def rows(number, running):
            block = mixed[pl.ds(pl.multiple_of(number * 16, 16), 16), cols].astype(F32)
            running = [r * s + block[:8] for r, s in zip(running, steps)]
            return tuple(r * s + block[8:] for r, s in zip(running, steps))

        empty = tuple(jnp.zeros((8, LANES), F32) for _ in range(POLES))
        running = lax.fori_loop(0, ROWS // 16, rows, empty, unroll=2)
        to = lanes(target_group * LANES, LANES)
        for pole in range(POLES):
            rate = decay_rates[pl.ds(pole, 1), cols]
            weighted = running[pole] * jnp.exp(-rate * (7.0 - sub))
            target[pl.ds(pole, 1), to] = jnp.sum(weighted, axis=0, keepdims=True)

    def medium_chunk(number, target):
        key_copies[number].wait_recv()

        @pl.when(seq == 0)
        def _():
            key_halo[number] = jnp.zeros((TAPS + EDGE, TILE), BF)

        if number == 0:
            value_copy.wait_recv()

            @pl.when(seq == 0)
            def _():
                value_halo[...] = jnp.zeros_like(value_halo)

            short_conv(value_own, value_halo, 2, value_tilde, EDGE)
        tile = chunk(1 - core, number)
        groups = TILE // LANES

        def state_group(n, _):
            end_states(tile * groups + n, target, number % half_tiles * groups + n)
            return 0

        run("medium", lambda: medium(number, tile))
        run("states", lambda: lax.fori_loop(0, groups, state_group, 0))

    for number in range(half_tiles):
        medium_chunk(number, states_away)
    states_copy = send(states_away, states_seen, {"seq": other})
    for number in range(half_tiles, tiles):
        medium_chunk(number, states_own)

    own_cols = lanes(core * half, half)
    rates = decay_rates[:, own_cols]
    block_decay = jnp.exp(-float(ROWS) * rates)
    states_copy.wait_recv()
    mine, theirs = states_own[...], states_seen[...]
    first = jnp.where(core == 0, mine, theirs)
    second = jnp.where(core == 0, theirs, mine)
    chip_total = block_decay * first + second
    chip_state[...] = chip_total.astype(BF)
    if n_y > 3:
        relayed(y_relay, n_y // 2)
    y_copies = [
        send(chip_state, chips_seen.at[step - 1], {"seq": along_y(step)}) for step in range(1, n_y)
    ]

    def long_local(tile, _):
        cols = lanes(tile * TILE, TILE)
        signal = mixed[:, cols]
        spec = mm(fwd_two[...], signal)
        x_re, x_im = spec[:HALF_TWO], spec[HALF_TWO:]
        k_re, k_im = kernel_spec[:HALF_TWO, cols], kernel_spec[HALF_TWO:, cols]
        re, im = x_re * k_re - x_im * k_im, x_re * k_im + x_im * k_re
        local_long[:, cols] = mm(inv_two[...], jnp.concatenate([re.astype(BF), im.astype(BF)], 0))
        return 0

    def kernel_spectrum(tile, _):
        cols = lanes(tile * TILE, TILE)
        high, low = split(long_kernel[:, cols])
        spec = mm(fwd_two[...], high) + mm(fwd_two[...], low)
        kernel_spec[:, cols] = spec * (1.0 / HALF_TWO)
        return 0

    run("kspec", lambda: lax.fori_loop(0, tiles, kernel_spectrum, 0))
    run("long1", lambda: lax.fori_loop(0, tiles // 2, long_local, 0))
    if n_z > 3:
        relayed(z_relay, 2)
    if n_z > 5:
        relay(z_relay, along_z, n_z, 3)

    chip_span = float(2 * ROWS)
    row_span = float(2 * ROWS * n_y)
    y_far = (n_y - 1 - y_pos).astype(F32)
    row_total = jnp.exp(-rates * (chip_span * y_far)) * chip_total
    before = jnp.zeros((POLES, half), F32)
    for step in range(1, n_y):
        y_copies[step - 1].wait_recv()
        seen = chips_seen[step - 1].astype(F32)
        source = (y_pos - step + n_y) % n_y
        distance = (n_y - 1 - source).astype(F32)
        row_total += jnp.exp(-rates * (chip_span * distance)) * seen
        before += jnp.where(y_pos >= step, jnp.exp(-rates * (chip_span * (step - 1))) * seen, 0.0)
    row_state[...] = row_total.astype(BF)
    if n_x > 3:
        relayed(x_relay, n_x // 2)
    x_copies = [
        send(row_state, rows_seen.at[step - 1], {"seq": along_x(step)}) for step in range(1, n_x)
    ]

    run("long2", lambda: lax.fori_loop(tiles // 2, tiles, long_local, 0))
    query_copy.wait_recv()

    @pl.when(seq == 0)
    def _():
        query_halo[...] = jnp.zeros_like(query_halo)

    run("query", lambda: short_conv(query_own, query_halo, 0, query_tilde, ROWS))
    squares[...] = jnp.zeros_like(squares)
    for step in range(3, n_z // 2 + 1):
        relayed(z_relay, step)
        if step < n_z // 2:
            relay(z_relay, along_z, n_z, step + 1)

    above = jnp.zeros((POLES, half), F32)
    for step in range(1, n_x):
        x_copies[step - 1].wait_recv()
        above += jnp.where(
            x_pos >= step,
            jnp.exp(-rates * (row_span * (step - 1))) * rows_seen[step - 1].astype(F32),
            0.0,
        )
    before += jnp.exp(-rates * (chip_span * y_pos.astype(F32))) * above
    after = block_decay * before + first
    carry_own[...] = jnp.where(core == 0, before, after)
    carry_away[...] = jnp.where(core == 0, after, before)
    carry_copy = send(carry_away, carry_seen, {"seq": other})


    def gate(group, carry, carry_group):
        cols = lanes(group * LANES, LANES)
        of = lanes(carry_group * LANES, LANES)
        steps = [eighth[pole, :, cols] for pole in range(POLES)]
        start = []
        for pole in range(POLES):
            one = pl.ds(pole, 1)
            weight = residues[one, cols] * carry[one, of] * jnp.exp(-decay_rates[one, cols])
            start.append(weight * powers[pole, :, cols])
        skip = skip_gain[:, cols]

        def rows(number, running):
            top = functools.reduce(jnp.add, running)
            running = [r * s for r, s in zip(running, steps)]
            low = functools.reduce(jnp.add, running)
            running = tuple(r * s for r, s in zip(running, steps))
            at = pl.ds(pl.multiple_of(number * 16, 16), 16)
            long_out = local_long[at, cols] + jnp.concatenate([top, low], 0)
            long_out = long_out.astype(BF).astype(F32)
            total = query_tilde[at, cols].astype(F32) * (
                long_out + skip * mixed[at, cols].astype(F32)
            )
            gated[at, cols] = total
            squares[at, :] += total * total
            return running

        lax.fori_loop(0, ROWS // 16, rows, tuple(start), unroll=4)

    def gate_half(side, carry):
        def one(n, _):
            gate(side * half_groups + n, carry, n)
            return 0

        run("gate", lambda: lax.fori_loop(0, half_groups, one, 0))

    gate_half(core, carry_own)
    carry_copy.wait_recv()
    gate_half(1 - core, carry_seen)

    row_sums[...] = jnp.sum(jnp.transpose(squares[...]), axis=0, keepdims=True)
    sum_copies = [
        send(row_sums, sums_seen.at[step - 1], along_z(step)) for step in range(1, n_z)
    ]
    total = row_sums[...]
    for step in range(1, n_z):
        sum_copies[step - 1].wait_recv()
        total = total + sums_seen[step - 1]
    scale = lax.rsqrt(total * (1.0 / (channels * n_z)) + 1e-05)
    scale = jnp.transpose(jnp.broadcast_to(scale, (LANES, ROWS)))

    def finish(group, _):
        cols = lanes(group * LANES, LANES)
        out[:, cols] = gated[:, cols] * scale * norm_gain[:, cols]
        return 0

    run("finish", lambda: lax.fori_loop(0, channels // LANES, finish, 0))
    for copy in sent:
        copy.wait_send()


def solution(mesh):
    n_seq, n_z = mesh.shape["seq"], mesh.shape["chan"]
    n_y = math.isqrt(n_seq // 2)
    n_x = n_seq // 2 // n_y
    tables = make_tables()

    def local(query, key, value, short_taps, medium_taps, residues, decay_rates, skip, gain):
        channels = query.shape[1]
        half = channels // 2
        operands = (
            query,
            key,
            value,
            short_taps,
            medium_taps,
            residues,
            decay_rates,
            skip.reshape(1, channels),
            gain.reshape(1, channels),
            *(jnp.asarray(table) for table in tables),
        )
        tiles = channels // TILE
        n_copies = tiles + 2 + 1 + (n_y - 1) + (n_x - 1) + 1 + (n_z - 1)
        vmem = pltpu.VMEM
        scratch = [
            vmem((ROWS, channels), BF),
            vmem((tiles, TAPS + EDGE, TILE), BF),
            vmem((ROWS, channels), BF),
            vmem((EDGE, channels), BF),
            vmem((ROWS, channels), BF),
            vmem((EDGE, channels), BF),
            vmem((EDGE + ROWS, TILE), F32),
            vmem((ROWS, channels), BF),
            vmem((ROWS, channels), BF),
            vmem((2 * HALF_ONE, channels), F32),
            vmem((2 * HALF_ONE, channels), F32),
            vmem((2 * HALF_TWO, channels), F32),
            vmem((ROWS, channels), F32),
            vmem((POLES, 8, channels), F32),
            vmem((POLES, 8, channels), F32),
            vmem((ROWS, channels), BF),
            vmem((POLES, half), F32),
            vmem((POLES, half), F32),
            vmem((POLES, half), F32),
            vmem((POLES, half), BF),
            vmem((n_y - 1, POLES, half), BF),
            vmem((POLES, half), BF),
            vmem((n_x - 1, POLES, half), BF),
            vmem((POLES, half), F32),
            vmem((POLES, half), F32),
            vmem((POLES, half), F32),
            vmem((ROWS, channels), F32),
            vmem((ROWS, channels), F32),
            vmem((ROWS, LANES), F32),
            vmem((1, ROWS), F32),
            vmem((n_z - 1, 1, ROWS), F32),
            pltpu.SemaphoreType.DMA((len(operands),)),
            pltpu.SemaphoreType.DMA((n_copies,)),
            pltpu.SemaphoreType.DMA((n_copies,)),
            *(
                pltpu.SemaphoreType.REGULAR((max(1, size // 2 - 1), 2))
                for size in (n_y, n_x, n_z)
            ),
        ]
        in_hbm = pl.BlockSpec(memory_space=pltpu.HBM)
        call = pl.pallas_call(
            functools.partial(kernel, (n_x, n_y, n_z, channels)),
            out_shape=jax.ShapeDtypeStruct((ROWS, channels), F32),
            in_specs=[in_hbm] * len(operands),
            out_specs=pl.BlockSpec(memory_space=pltpu.VMEM),
            scratch_shapes=[vmem(x.shape, x.dtype) for x in operands[3:]] + scratch,
            compiler_params=pltpu.CompilerParams(
                collective_id=0, has_side_effects=True, vmem_limit_bytes=60 * 1024 * 1024
            ),
        )
        return call(*operands).astype(BF)

    in_specs = (
        P("seq", "chan"),
        P("seq", "chan"),
        P("seq", "chan"),
        P(None, None, "chan"),
        P(None, "chan"),
        P(None, "chan"),
        P(None, "chan"),
        P("chan"),
        P("chan"),
    )
    return jax.shard_map(
        local, mesh=mesh, in_specs=in_specs, out_specs=P("seq", "chan"), check_vma=False
    )
```

time: 38.7 us -> 34.4 us (0.89)
  Pallas kernels: 36.7 us -> 32.2 us
  other arithmetic: 0 us -> 2.1 us
  local copies, waits for them, and re-layouts: 1.87 us -> 0 us
    pallas_call x1, Pallas kernels: 36.7 us -> 32.2 us  [local(): return call(*operands).astype(BF)]
    convert_element_type x0 -> x1, other arithmetic: none -> 2.1 us  [local(): return call(*operands).astype(BF)]
    unnamed x1 -> x0, local copies, waits for them, and re-layouts: 1.87 us -> none
where the time goes in v2:
time: 34.4 us; the launch traced here: 34.3 us
  Pallas kernels  32.2 us (94%)
  other arithmetic  2.1 us (6%)
    pallas_call x1, Pallas kernels, local(): return call(*operands).astype(BF)  32.2 us
    convert_element_type x1, other arithmetic, local(): return call(*operands).astype(BF)  2.1 us

profile of v2, /device:TPU:1, one launch (start us, length us, event | category | flops | bytes accessed | tf_op | source)
XLA Modules:
  0.0 34.3 jit_solution(8754738419268322977)
XLA Ops:
  0.0 32.2 %shard_map.136 = f32[256,1024]{1,0:T(8,128)} custom-call(bf16[256,1024]{1,0:T(8,128)(2,1)} %query.1, bf16[256,1024]{1,0:T(8,128)(2,1)} %key.1, bf16[256,1024]{1,0:T(8,128)(2,1)} %value.1, bf16[3,3,1024]{2,1,0:T(4,128)(2,1)} %rest_0_.1, bf16[128,1024]{1,0:T(8,128)(2,1)} %rest_1_.1, f32[16,1024]{1,0:T(8,128)} %rest_2_.1, f32[16,1024]{1,0:T(8,128)} %rest_3_.1, ...), custom_call_target="tpu_custom_call" | custom-call | tf_op jit(solution)/shard_map/pallas_call | solution.py:599
  32.2 2.1 %convert_element_type.3 = bf16[256,1024]{1,0:T(8,128)(2,1)} convert(f32[256,1024]{1,0:T(8,128)} %shard_map.136) | non-fusion elementwise | flops 262144 | bytes 1572864 | tf_op jit(solution)/shard_map/convert_element_type | solution.py:599

commit v3 on v2

--- a/solution.py
+++ b/solution.py
@@ -53,6 +53,11 @@
 
 def run(name, task):
     task()
+
+
+def distance(offset, n_x, n_y):
+    down, across = divmod(offset, n_y)
+    return min(down, n_x - down) + min(across, n_y - across)
 
 
 def split(value):
@@ -104,13 +109,13 @@
     states_seen,
     chip_state,
     chips_seen,
-    row_state,
-    rows_seen,
+    before_ref,
     carry_own,
     carry_away,
     carry_seen,
     local_long,
     gated,
+    query_wide,
     squares,
     row_sums,
     sums_seen,
@@ -120,6 +125,9 @@
     y_relay,
     x_relay,
     z_relay,
+    plane_sems,
+    chip_send,
+    chip_recv,
 ):
     n_x, n_y, n_z, channels = dims
     (
@@ -206,12 +214,13 @@
     def seq_x(step):
         return {"seq": along_x(step)}
 
-    for step in range(2, n_y // 2 + 1):
-        relay(y_relay, seq_y, n_y, step)
-        relayed(y_relay, step) if step < n_y // 2 else None
-    for step in range(2, n_x // 2 + 1):
-        relay(x_relay, seq_x, n_x, step)
-        relayed(x_relay, step) if step < n_x // 2 else None
+    def chip(position):
+        return {"seq": position * 2 + core}
+
+    if n_y > 3:
+        relay(y_relay, seq_y, n_y, 2)
+    if n_x > 3:
+        relay(x_relay, seq_x, n_x, 2)
     if n_z > 3:
         relay(z_relay, along_z, n_z, 2)
 
@@ -290,6 +299,15 @@
         load.wait()
     run("value", lambda: short_conv(value_own, None, 2, value_tilde, ROWS))
 
+    if n_y > 3:
+        relayed(y_relay, 2)
+    if n_x > 3:
+        relayed(x_relay, 2)
+    for step in range(1, n_x):
+        pl.semaphore_signal(
+            plane_sems.at[step - 1], inc=1, device_id=seq_x(step), device_id_type=MESH
+        )
+
     def pole_kernel(group, _):
         cols = lanes(group * LANES, LANES)
         steps = [eighth[pole, :, cols] for pole in range(POLES)]
@@ -307,6 +325,9 @@
 
     for load in loads[8:]:
         load.wait()
+    if n_z > 5:
+        relayed(z_relay, 2)
+        relay(z_relay, along_z, n_z, 3)
 
     def medium(number, tile):
         cols = lanes(tile * TILE, TILE)
@@ -374,6 +395,10 @@
     for number in range(half_tiles, tiles):
         medium_chunk(number, states_own)
 
+    for step in range(3, n_z // 2):
+        relayed(z_relay, step)
+        relay(z_relay, along_z, n_z, step + 1)
+
     own_cols = lanes(core * half, half)
     rates = decay_rates[:, own_cols]
     block_decay = jnp.exp(-float(ROWS) * rates)
@@ -381,13 +406,24 @@
     mine, theirs = states_own[...], states_seen[...]
     first = jnp.where(core == 0, mine, theirs)
     second = jnp.where(core == 0, theirs, mine)
-    chip_total = block_decay * first + second
-    chip_state[...] = chip_total.astype(BF)
-    if n_y > 3:
-        relayed(y_relay, n_y // 2)
-    y_copies = [
-        send(chip_state, chips_seen.at[step - 1], {"seq": along_y(step)}) for step in range(1, n_y)
-    ]
+    chip_state[...] = (block_decay * first + second).astype(BF)
+    for step in range(1, n_x):
+        pl.semaphore_wait(plane_sems.at[step - 1], 1)
+    n_chips = n_x * n_y
+    position = seq // 2
+    offsets = sorted(range(1, n_chips), key=lambda n: -distance(n, n_x, n_y))
+    chip_copies = []
+    for offset in offsets:
+        copy = pltpu.make_async_remote_copy(
+            src_ref=chip_state,
+            dst_ref=chips_seen.at[position],
+            send_sem=chip_send.at[offset],
+            recv_sem=chip_recv.at[position],
+            device_id=chip(lax.rem(position + offset, n_chips)),
+            device_id_type=MESH,
+        )
+        pl.when(position + offset < n_chips)(copy.start)
+        chip_copies.append((offset, copy))
 
     def long_local(tile, _):
         cols = lanes(tile * TILE, TILE)
@@ -406,31 +442,16 @@
         kernel_spec[:, cols] = spec * (1.0 / HALF_TWO)
         return 0
 
+    def pregate(group, _):
+        cols = lanes(group * LANES, LANES)
+        long_part = local_long[:, cols] + skip_gain[:, cols] * mixed[:, cols].astype(F32)
+        wide = query_tilde[:, cols].astype(F32)
+        query_wide[:, cols] = wide
+        gated[:, cols] = wide * long_part
+        return 0
+
     run("kspec", lambda: lax.fori_loop(0, tiles, kernel_spectrum, 0))
     run("long1", lambda: lax.fori_loop(0, tiles // 2, long_local, 0))
-    if n_z > 3:
-        relayed(z_relay, 2)
-    if n_z > 5:
-        relay(z_relay, along_z, n_z, 3)
-
-    chip_span = float(2 * ROWS)
-    row_span = float(2 * ROWS * n_y)
-    y_far = (n_y - 1 - y_pos).astype(F32)
-    row_total = jnp.exp(-rates * (chip_span * y_far)) * chip_total
-    before = jnp.zeros((POLES, half), F32)
-    for step in range(1, n_y):
-        y_copies[step - 1].wait_recv()
-        seen = chips_seen[step - 1].astype(F32)
-        source = (y_pos - step + n_y) % n_y
-        distance = (n_y - 1 - source).astype(F32)
-        row_total += jnp.exp(-rates * (chip_span * distance)) * seen
-        before += jnp.where(y_pos >= step, jnp.exp(-rates * (chip_span * (step - 1))) * seen, 0.0)
-    row_state[...] = row_total.astype(BF)
-    if n_x > 3:
-        relayed(x_relay, n_x // 2)
-    x_copies = [
-        send(row_state, rows_seen.at[step - 1], {"seq": along_x(step)}) for step in range(1, n_x)
-    ]
 
     run("long2", lambda: lax.fori_loop(tiles // 2, tiles, long_local, 0))
     query_copy.wait_recv()
@@ -440,21 +461,26 @@
         query_halo[...] = jnp.zeros_like(query_halo)
 
     run("query", lambda: short_conv(query_own, query_halo, 0, query_tilde, ROWS))
+    run("pregate", lambda: lax.fori_loop(0, channels // LANES, pregate, 0))
     squares[...] = jnp.zeros_like(squares)
-    for step in range(3, n_z // 2 + 1):
-        relayed(z_relay, step)
-        if step < n_z // 2:
-            relay(z_relay, along_z, n_z, step + 1)
-
-    above = jnp.zeros((POLES, half), F32)
-    for step in range(1, n_x):
-        x_copies[step - 1].wait_recv()
-        above += jnp.where(
-            x_pos >= step,
-            jnp.exp(-rates * (row_span * (step - 1))) * rows_seen[step - 1].astype(F32),
-            0.0,
-        )
-    before += jnp.exp(-rates * (chip_span * y_pos.astype(F32))) * above
+
+    chip_decay = jnp.exp(-float(2 * ROWS) * rates)
+    before_ref[...] = jnp.zeros_like(before_ref)
+    for source in range(n_chips - 1):
+
+        @pl.when(source < position)
+        def _():
+            pltpu.make_async_remote_copy(
+                src_ref=chip_state,
+                dst_ref=chips_seen.at[source],
+                send_sem=chip_send.at[0],
+                recv_sem=chip_recv.at[source],
+                device_id=chip(position),
+                device_id_type=MESH,
+            ).wait_recv()
+            before_ref[...] = before_ref[...] * chip_decay + chips_seen[source].astype(F32)
+
+    before = before_ref[...]
     after = block_decay * before + first
     carry_own[...] = jnp.where(core == 0, before, after)
     carry_away[...] = jnp.where(core == 0, after, before)
@@ -470,7 +496,6 @@
             one = pl.ds(pole, 1)
             weight = residues[one, cols] * carry[one, of] * jnp.exp(-decay_rates[one, cols])
             start.append(weight * powers[pole, :, cols])
-        skip = skip_gain[:, cols]
 
         def rows(number, running):
             top = functools.reduce(jnp.add, running)
@@ -478,11 +503,7 @@
             low = functools.reduce(jnp.add, running)
             running = tuple(r * s for r, s in zip(running, steps))
             at = pl.ds(pl.multiple_of(number * 16, 16), 16)
-            long_out = local_long[at, cols] + jnp.concatenate([top, low], 0)
-            long_out = long_out.astype(BF).astype(F32)
-            total = query_tilde[at, cols].astype(F32) * (
-                long_out + skip * mixed[at, cols].astype(F32)
-            )
+            total = gated[at, cols] + query_wide[at, cols] * jnp.concatenate([top, low], 0)
             gated[at, cols] = total
             squares[at, :] += total * total
             return running
@@ -501,6 +522,8 @@
     gate_half(1 - core, carry_seen)
 
     row_sums[...] = jnp.sum(jnp.transpose(squares[...]), axis=0, keepdims=True)
+    if n_z > 3:
+        relayed(z_relay, n_z // 2)
     sum_copies = [
         send(row_sums, sums_seen.at[step - 1], along_z(step)) for step in range(1, n_z)
     ]
@@ -513,12 +536,14 @@
 
     def finish(group, _):
         cols = lanes(group * LANES, LANES)
-        out[:, cols] = gated[:, cols] * scale * norm_gain[:, cols]
+        out[:, cols] = (gated[:, cols] * scale * norm_gain[:, cols]).astype(BF)
         return 0
 
     run("finish", lambda: lax.fori_loop(0, channels // LANES, finish, 0))
     for copy in sent:
         copy.wait_send()
+    for offset, copy in chip_copies:
+        pl.when(position + offset < n_chips)(copy.wait_send)
 
 
 def solution(mesh):
@@ -543,7 +568,7 @@
             *(jnp.asarray(table) for table in tables),
         )
         tiles = channels // TILE
-        n_copies = tiles + 2 + 1 + (n_y - 1) + (n_x - 1) + 1 + (n_z - 1)
+        n_copies = tiles + 2 + 1 + 1 + (n_z - 1)
         vmem = pltpu.VMEM
         scratch = [
             vmem((ROWS, channels), BF),
@@ -566,12 +591,12 @@
             vmem((POLES, half), F32),
             vmem((POLES, half), F32),
             vmem((POLES, half), BF),
-            vmem((n_y - 1, POLES, half), BF),
-            vmem((POLES, half), BF),
-            vmem((n_x - 1, POLES, half), BF),
+            vmem((n_x * n_y, POLES, half), BF),
             vmem((POLES, half), F32),
             vmem((POLES, half), F32),
             vmem((POLES, half), F32),
+            vmem((POLES, half), F32),
+            vmem((ROWS, channels), F32),
             vmem((ROWS, channels), F32),
             vmem((ROWS, channels), F32),
             vmem((ROWS, LANES), F32),
@@ -584,11 +609,14 @@
                 pltpu.SemaphoreType.REGULAR((max(1, size // 2 - 1), 2))
                 for size in (n_y, n_x, n_z)
             ),
+            pltpu.SemaphoreType.REGULAR((n_x,)),
+            pltpu.SemaphoreType.DMA((n_x * n_y,)),
+            pltpu.SemaphoreType.DMA((n_x * n_y,)),
         ]
         in_hbm = pl.BlockSpec(memory_space=pltpu.HBM)
         call = pl.pallas_call(
             functools.partial(kernel, (n_x, n_y, n_z, channels)),
-            out_shape=jax.ShapeDtypeStruct((ROWS, channels), F32),
+            out_shape=pltpu.VMEM((ROWS, channels), BF),
             in_specs=[in_hbm] * len(operands),
             out_specs=pl.BlockSpec(memory_space=pltpu.VMEM),
             scratch_shapes=[vmem(x.shape, x.dtype) for x in operands[3:]] + scratch,
@@ -596,7 +624,7 @@
                 collective_id=0, has_side_effects=True, vmem_limit_bytes=60 * 1024 * 1024
             ),
         )
-        return call(*operands).astype(BF)
+        return call(*(pltpu.with_memory_space_constraint(x, pltpu.HBM) for x in operands))
 
     in_specs = (
         P("seq", "chan"),

time: 34.4 us -> 30.2 us (0.88)
  Pallas kernels: 32.2 us -> 29.3 us
  other arithmetic: 2.1 us -> 0 us
  local copies, waits for them, and re-layouts: 0 us -> 0.8 us
    pallas_call x1, Pallas kernels: 32.2 us -> 29.3 us  [local(): call(*(pltpu.with_memory_space_constraint(x, pltpu.HBM) for x in operands))]
    convert_element_type x1 -> x0, other arithmetic: 2.1 us -> none  [local(): return call(*operands).astype(BF)]
    unnamed x0 -> x1, local copies, waits for them, and re-layouts: none -> 0.8 us
where the time goes in v3:
time: 30.2 us; the launch traced here: 30.1 us
  Pallas kernels  29.3 us (97%)
  local copies, waits for them, and re-layouts  0.8 us (3%)
    pallas_call x1, Pallas kernels, local(): call(*(pltpu.with_memory_space_constraint(x, pltpu.HBM) for x in operands))  29.3 us
    unnamed x1, local copies, waits for them, and re-layouts  0.8 us

profile of v3, /device:TPU:1, one launch (start us, length us, event | category | flops | bytes accessed | tf_op | source)
XLA Modules:
  0.0 30.1 jit_solution(16508461752476505804)
XLA Ops:
  0.0 29.3 %shard_map.136 = bf16[256,1024]{1,0:T(8,128)(2,1)S(1)} custom-call(bf16[256,1024]{1,0:T(8,128)(2,1)} %query.1, bf16[256,1024]{1,0:T(8,128)(2,1)} %key.1, bf16[256,1024]{1,0:T(8,128)(2,1)} %value.1, bf16[3,3,1024]{2,1,0:T(4,128)(2,1)} %rest_0_.1, bf16[128,1024]{1,0:T(8,128)(2,1)} %rest_1_.1, f32[16,1024]{1,0:T(8,128)} %rest_2_.1, f32[16,1024]{1,0:T(8,128)} %rest_3_.1, ...), custom_call_target="tpu_custom_call" | custom-call | tf_op jit(solution)/shard_map/pallas_call | solution.py:627
  29.3 0.8 %copy.16 = bf16[256,1024]{1,0:T(8,128)(2,1)} copy(bf16[256,1024]{1,0:T(8,128)(2,1)S(1)} %shard_map.136) | data formatting | bytes 1048576

commit v4 on v3

--- a/solution.py
+++ b/solution.py
@@ -60,6 +60,14 @@
     return min(down, n_x - down) + min(across, n_y - across)
 
 
+def next_two(running, steps):
+    now = functools.reduce(jnp.add, running)
+    later = running[0] * steps[0]
+    for state, step in zip(running[1:], steps[1:]):
+        later = later + state * step
+    return jnp.concatenate([now, later], 0)
+
+
 def split(value):
     high = value.astype(BF)
     return high, (value - high.astype(F32)).astype(BF)
@@ -91,9 +99,11 @@
     key_own,
     key_halo,
     value_own,
-    value_halo,
+    edge_sent,
+    edge_seen,
     query_own,
-    query_halo,
+    query_sent,
+    query_seen,
     staged,
     value_tilde,
     query_tilde,
@@ -102,6 +112,8 @@
     kernel_spec,
     long_kernel,
     powers,
+    reverse,
+    first_weight,
     eighth,
     mixed,
     states_own,
@@ -166,9 +178,8 @@
     def along_x(step):
         return (((x_pos + step) % n_x) * n_y + y_pos) * 2 + core
 
-    pairs = [(sources[n], buffers[n]) for n in (3, 6, 1, 0, 10)] + [(key, key_own)]
-    pairs += [(value, value_own)] + [(sources[n], buffers[n]) for n in (2, 7, 8, 9, 4, 5)]
-    pairs += [(query, query_own)]
+    pairs = [(sources[3], decay_rates), (key, key_own), (value, value_own), (query, query_own)]
+    pairs += [(sources[n], buffers[n]) for n in (6, 1, 0, 10, 2, 8, 7, 9, 4, 5)]
     loads = [
         pltpu.make_async_copy(source, target, load_sems.at[number])
         for number, (source, target) in enumerate(pairs)
@@ -192,6 +203,7 @@
         for pole in range(POLES):
             rate = decay_rates[pl.ds(pole, 1), cols]
             powers[pole, :, cols] = jnp.exp(-rate * sub)
+            reverse[pole, :, cols] = jnp.exp(-rate * (7.0 - sub))
             eighth[pole, :, cols] = jnp.broadcast_to(jnp.exp(-8.0 * rate), (8, LANES))
         return 0
 
@@ -247,17 +259,25 @@
     def chunk(side, number):
         return (side if number < half_tiles else 1 - side) * half_tiles + number % half_tiles
 
+    def last_rows(source, end, count):
+        return source[end - EDGE : end, :].astype(F32)[EDGE - count :]
+
     key_copies = []
-    for number in range(tiles):
-        piece = key.at[
-            pl.ds(ROWS - TAPS - EDGE, TAPS + EDGE), lanes(chunk(core, number) * TILE, TILE)
-        ]
+
+    def send_chunk():
+        number = len(key_copies)
+        piece = key.at[pl.ds(ROWS - TAPS, TAPS), lanes(chunk(core, number) * TILE, TILE)]
         key_copies.append(send(piece, key_halo.at[number], {"seq": right}))
-        if number == 0:
-            value_copy = send(value.at[pl.ds(ROWS - EDGE, EDGE), :], value_halo, {"seq": right})
-    query_copy = send(query.at[pl.ds(ROWS - EDGE, EDGE), :], query_halo, {"seq": right})
-
-    for load in loads[1:6]:
+
+    send_chunk()
+    for load in loads[1:4]:
+        load.wait()
+    edge_sent[0:2, :] = last_rows(value_own, ROWS, 2)
+    edge_sent[2:3, :] = last_rows(key_own, ROWS - TAPS, 1)
+    edge_sent[3:4, :] = jnp.zeros((1, channels), F32)
+    query_sent[...] = last_rows(query_own, ROWS, 2)
+    edge_copy = send(edge_sent, edge_seen, {"seq": right})
+    for load in loads[4:8]:
         load.wait()
 
     def before_halo(tile, _):
@@ -274,15 +294,25 @@
         key_spec[:, cols] = mm(fwd_one[:, TAPS:], key_own[:, cols])
         return 0
 
-    run("before", lambda: lax.fori_loop(0, channels // TILE, before_halo, 0))
-
-    def short_conv(source, halo, taps_row, target, count):
+    def before_half(number):
+        run(
+            "before",
+            lambda: lax.fori_loop(
+                number * half_tiles, (number + 1) * half_tiles, before_halo, 0, unroll=True
+            ),
+        )
+
+    before_half(0)
+    send_chunk()
+    before_half(1)
+    send_chunk()
+
+    def short_conv(source, halo, taps_row, target, count, first=0, last=tiles):
         def one(tile, _):
             cols = lanes(tile * TILE, TILE)
-            if halo is None:
-                staged[0:EDGE, :] = jnp.zeros((EDGE, TILE), F32)
-            else:
-                staged[0:EDGE, :] = halo[:, cols].astype(F32)
+            staged[0:EDGE, :] = jnp.zeros((EDGE, TILE), F32)
+            if halo is not None:
+                staged[EDGE - 2 : EDGE, :] = halo[0:2, cols]
             staged[EDGE : EDGE + count, :] = source[0:count, cols].astype(F32)
             weights = short_taps[taps_row, :, cols].astype(F32)
             total = (
@@ -293,11 +323,12 @@
             target[0:count, cols] = total.astype(BF)
             return 0
 
-        lax.fori_loop(0, tiles, one, 0)
-
-    for load in loads[6:8]:
-        load.wait()
+        lax.fori_loop(first, last, one, 0)
+
     run("value", lambda: short_conv(value_own, None, 2, value_tilde, ROWS))
+    while len(key_copies) < tiles:
+        send_chunk()
+    query_copy = send(query_sent, query_seen, {"seq": right})
 
     if n_y > 3:
         relayed(y_relay, 2)
@@ -308,22 +339,26 @@
             plane_sems.at[step - 1], inc=1, device_id=seq_x(step), device_id_type=MESH
         )
 
+    loads[8].wait()
+
     def pole_kernel(group, _):
         cols = lanes(group * LANES, LANES)
         steps = [eighth[pole, :, cols] for pole in range(POLES)]
         start = [residues[pl.ds(pole, 1), cols] * powers[pole, :, cols] for pole in range(POLES)]
+        twice = [step * step for step in steps]
 
         def rows(number, running):
-            total = functools.reduce(jnp.add, running)
-            long_kernel[pl.ds(pl.multiple_of(number * 8, 8), 8), cols] = total
-            return tuple(r * s for r, s in zip(running, steps))
-
-        lax.fori_loop(0, ROWS // 8, rows, tuple(start), unroll=4)
+            at = pl.ds(pl.multiple_of(number * 16, 16), 16)
+            long_kernel[at, cols] = next_two(running, steps)
+            return tuple(r * s for r, s in zip(running, twice))
+
+        lax.fori_loop(0, ROWS // 16, rows, tuple(start), unroll=4)
         return 0
 
+    first_weight[...] = residues[...] * jnp.exp(-decay_rates[...])
     run("kernel", lambda: lax.fori_loop(0, channels // LANES, pole_kernel, 0))
 
-    for load in loads[8:]:
+    for load in loads[9:]:
         load.wait()
     if n_z > 5:
         relayed(z_relay, 2)
@@ -331,7 +366,7 @@
 
     def medium(number, tile):
         cols = lanes(tile * TILE, TILE)
-        spec = key_spec[:, cols] + mm(fwd_one[:, :TAPS], key_halo[number, EDGE:])
+        spec = key_spec[:, cols] + mm(fwd_one[:, :TAPS], key_halo[number])
         x_re, x_im = spec[:HALF_ONE], spec[HALF_ONE:]
         t_re, t_im = tap_spec[:HALF_ONE, cols], tap_spec[HALF_ONE:, cols]
         re, im = x_re * t_re - x_im * t_im, x_re * t_im + x_im * t_re
@@ -340,7 +375,7 @@
             EDGE - 1 :
         ]
         ends = (
-            key_halo[number, :EDGE].astype(F32)[EDGE - 1 :]
+            edge_seen[2:3, cols]
             + key_own[ROWS - EDGE :, cols].astype(F32)[EDGE - 1 :]
         )
         row = lax.broadcasted_iota(jnp.int32, (ROWS, TILE), 0)
@@ -360,8 +395,7 @@
         running = lax.fori_loop(0, ROWS // 16, rows, empty, unroll=2)
         to = lanes(target_group * LANES, LANES)
         for pole in range(POLES):
-            rate = decay_rates[pl.ds(pole, 1), cols]
-            weighted = running[pole] * jnp.exp(-rate * (7.0 - sub))
+            weighted = running[pole] * reverse[pole, :, cols]
             target[pl.ds(pole, 1), to] = jnp.sum(weighted, axis=0, keepdims=True)
 
     def medium_chunk(number, target):
@@ -369,16 +403,16 @@
 
         @pl.when(seq == 0)
         def _():
-            key_halo[number] = jnp.zeros((TAPS + EDGE, TILE), BF)
+            key_halo[number] = jnp.zeros((TAPS, TILE), BF)
 
         if number == 0:
-            value_copy.wait_recv()
+            edge_copy.wait_recv()
 
             @pl.when(seq == 0)
             def _():
-                value_halo[...] = jnp.zeros_like(value_halo)
-
-            short_conv(value_own, value_halo, 2, value_tilde, EDGE)
+                edge_seen[...] = jnp.zeros_like(edge_seen)
+
+            short_conv(value_own, edge_seen, 2, value_tilde, EDGE)
         tile = chunk(1 - core, number)
         groups = TILE // LANES
 
@@ -450,17 +484,17 @@
         gated[:, cols] = wide * long_part
         return 0
 
-    run("kspec", lambda: lax.fori_loop(0, tiles, kernel_spectrum, 0))
-    run("long1", lambda: lax.fori_loop(0, tiles // 2, long_local, 0))
-
-    run("long2", lambda: lax.fori_loop(tiles // 2, tiles, long_local, 0))
+    run("kspec", lambda: lax.fori_loop(0, tiles, kernel_spectrum, 0, unroll=True))
+    run("long1", lambda: lax.fori_loop(0, tiles // 2, long_local, 0, unroll=True))
+
+    run("long2", lambda: lax.fori_loop(tiles // 2, tiles, long_local, 0, unroll=True))
     query_copy.wait_recv()
 
     @pl.when(seq == 0)
     def _():
-        query_halo[...] = jnp.zeros_like(query_halo)
-
-    run("query", lambda: short_conv(query_own, query_halo, 0, query_tilde, ROWS))
+        query_seen[...] = jnp.zeros_like(query_seen)
+
+    run("query", lambda: short_conv(query_own, query_seen, 0, query_tilde, ROWS))
     run("pregate", lambda: lax.fori_loop(0, channels // LANES, pregate, 0))
     squares[...] = jnp.zeros_like(squares)
 
@@ -491,22 +525,16 @@
         cols = lanes(group * LANES, LANES)
         of = lanes(carry_group * LANES, LANES)
         steps = [eighth[pole, :, cols] for pole in range(POLES)]
-        start = []
-        for pole in range(POLES):
-            one = pl.ds(pole, 1)
-            weight = residues[one, cols] * carry[one, of] * jnp.exp(-decay_rates[one, cols])
-            start.append(weight * powers[pole, :, cols])
+        weight = first_weight[:, cols] * carry[:, of]
+        start = [weight[pole : pole + 1] * powers[pole, :, cols] for pole in range(POLES)]
+        twice = [step * step for step in steps]
 
         def rows(number, running):
-            top = functools.reduce(jnp.add, running)
-            running = [r * s for r, s in zip(running, steps)]
-            low = functools.reduce(jnp.add, running)
-            running = tuple(r * s for r, s in zip(running, steps))
             at = pl.ds(pl.multiple_of(number * 16, 16), 16)
-            total = gated[at, cols] + query_wide[at, cols] * jnp.concatenate([top, low], 0)
+            total = gated[at, cols] + query_wide[at, cols] * next_two(running, steps)
             gated[at, cols] = total
             squares[at, :] += total * total
-            return running
+            return tuple(r * s for r, s in zip(running, twice))
 
         lax.fori_loop(0, ROWS // 16, rows, tuple(start), unroll=4)
 
@@ -572,11 +600,13 @@
         vmem = pltpu.VMEM
         scratch = [
             vmem((ROWS, channels), BF),
-            vmem((tiles, TAPS + EDGE, TILE), BF),
+            vmem((tiles, TAPS, TILE), BF),
             vmem((ROWS, channels), BF),
-            vmem((EDGE, channels), BF),
+            vmem((4, channels), F32),
+            vmem((4, channels), F32),
             vmem((ROWS, channels), BF),
-            vmem((EDGE, channels), BF),
+            vmem((2, channels), F32),
+            vmem((2, channels), F32),
             vmem((EDGE + ROWS, TILE), F32),
             vmem((ROWS, channels), BF),
             vmem((ROWS, channels), BF),
@@ -585,6 +615,8 @@
             vmem((2 * HALF_TWO, channels), F32),
             vmem((ROWS, channels), F32),
             vmem((POLES, 8, channels), F32),
+            vmem((POLES, 8, channels), F32),
+            vmem((POLES, channels), F32),
             vmem((POLES, 8, channels), F32),
             vmem((ROWS, channels), BF),
             vmem((POLES, half), F32),

time: 30.2 us -> 28.6 us (0.947)
  the two profiles are of different devices: /device:TPU:1 before, /device:TPU:2 now
where the time goes in v4:
time: 28.6 us; the launch traced here: 28.5 us
  Pallas kernels  27.7 us (97%)
  local copies, waits for them, and re-layouts  0.8 us (3%)
    pallas_call x1, Pallas kernels, local(): call(*(pltpu.with_memory_space_constraint(x, pltpu.HBM) for x in operands))  27.7 us
    unnamed x1, local copies, waits for them, and re-layouts  0.8 us

profile of v4, /device:TPU:2, one launch (start us, length us, event | category | flops | bytes accessed | tf_op | source)
XLA Modules:
  0.0 28.5 jit_solution(12139399561796815056)
XLA Ops:
  0.0 27.7 %shard_map.136 = bf16[256,1024]{1,0:T(8,128)(2,1)S(1)} custom-call(bf16[256,1024]{1,0:T(8,128)(2,1)} %query.1, bf16[256,1024]{1,0:T(8,128)(2,1)} %key.1, bf16[256,1024]{1,0:T(8,128)(2,1)} %value.1, bf16[3,3,1024]{2,1,0:T(4,128)(2,1)} %rest_0_.1, bf16[128,1024]{1,0:T(8,128)(2,1)} %rest_1_.1, f32[16,1024]{1,0:T(8,128)} %rest_2_.1, f32[16,1024]{1,0:T(8,128)} %rest_3_.1, ...), custom_call_target="tpu_custom_call" | custom-call | tf_op jit(solution)/shard_map/pallas_call | solution.py:659
  27.8 0.8 %copy.16 = bf16[256,1024]{1,0:T(8,128)(2,1)} copy(bf16[256,1024]{1,0:T(8,128)(2,1)S(1)} %shard_map.136) | data formatting | bytes 1048576
